TPU v7x, 512 devices: a whole 4x4x16 slice. The times are simulated.
512 devices in a mesh: ens: 16 (over y, z_hi), sp: 32 (over x, z_lo, core).
Axes of the slice: x: 4, y: 4, z: 16 (z_hi: 4, z_lo: 4; z = z_hi * 4 + z_lo), core: 2. Of those that a mesh axis runs over, the one named last changes fastest.
Arguments:
- embedding: bfloat16 [16, 192, 384, 256], P('ens', 'sp'), may hold values from -6 to 6
- target: bfloat16 [24, 192, 384], P(None, 'sp'), may hold values from -6 to 6
- gain: float32 [256], replicated, may hold values from 0.5 to 1.5
- head_w: bfloat16 [256, 24], replicated, may hold values from -0.375 to 0.375
Outputs:
- grad_head_w: float32 [256, 24], replicated
- grad_gain: float32 [256], replicated
All inputs are finite; a program needn't handle non-finite values.
Results may differ from a plain program's by a relative error of at most 0.0049.
The roundings to bfloat16 on the way count: a program that leaves them out, or rounds other values in their place, can miss the bound.
Values sent between devices are 32-bit elements; how exact they have to be, the bound alone decides.
A program may use at most 64 MiB of HBM per device.

v0:
```python
import math

import jax
import jax.numpy as jnp
from jax import lax
from jax.sharding import PartitionSpec as P

EMBED_CHANNELS = 256
NVAR = 24
LATITUDE_ROWS = 192
LONGITUDE_COLUMNS = 384
MMAX = 192
LMAX = 192


def dft_table():
    column = jnp.arange(LONGITUDE_COLUMNS, dtype=jnp.int32)
    wave = jnp.arange(MMAX, dtype=jnp.int32)
    phase = column[:, None] * wave[None, :] % LONGITUDE_COLUMNS
    angle = phase.astype(jnp.float32) * (2.0 * math.pi / LONGITUDE_COLUMNS)
    factor = 2.0 * math.pi / LONGITUDE_COLUMNS
    return (jnp.stack([jnp.cos(angle), -jnp.sin(angle)], axis=2) * factor).reshape(
        LONGITUDE_COLUMNS, 2 * MMAX
    )


def block_length(total):
    best = 1
    target_len = math.sqrt(total)
    for option in range(1, total + 1):
        if total % option == 0 and abs(option - target_len) < abs(best - target_len):
            best = option
    return best


def legendre_rows(m_first, count):
    rows = jnp.arange(LATITUDE_ROWS, dtype=jnp.int32).astype(jnp.float32)
    theta = math.pi * (rows + 0.5) / LATITUDE_ROWS
    cosine = jnp.cos(theta)
    sine = jnp.sin(theta)
    steps_q = jnp.arange(1, MMAX, dtype=jnp.int32).astype(jnp.float32)
    terms = jnp.log((2.0 * steps_q - 1.0) / (2.0 * steps_q))
    running = jnp.concatenate([jnp.zeros((1,), jnp.float32), jnp.cumsum(terms)])
    partial_sum = lax.dynamic_slice_in_dim(running, m_first, count)
    waves = (m_first + jnp.arange(count, dtype=jnp.int32)).astype(jnp.float32)[:, None]
    diagonal = jnp.exp(
        0.5 * jnp.log((2.0 * waves + 1.0) / (4.0 * math.pi))
        + 0.5 * partial_sum[:, None]
        + waves * jnp.log(sine)[None, :]
    )
    weight = (
        math.pi
        / LATITUDE_ROWS
        * sine
        * math.sqrt(LATITUDE_ROWS * LONGITUDE_COLUMNS / (4.0 * math.pi))
    )
    piece = block_length(LMAX)
    blocks = LMAX // piece
    wave_grid = waves[None]
    cos_grid = cosine[None, None, :]
    block_base = (jnp.arange(blocks, dtype=jnp.int32) * piece)[:, None, None]

    def factors(step):
        deg = (block_base + step).astype(jnp.float32)
        first = jnp.sqrt(
            (4.0 * deg * deg - 1.0) / jnp.maximum(deg * deg - wave_grid * wave_grid, 1.0)
        )
        second = jnp.sqrt(
            jnp.maximum((deg - 1.0) ** 2 - wave_grid * wave_grid, 0.0)
            / jnp.maximum(4.0 * (deg - 1.0) ** 2 - 1.0, 1.0)
        )
        above = deg > wave_grid
        lead = jnp.where(above, first * cos_grid, 0.0)
        lag = jnp.where(above, -first * second, 0.0)
        offset = jnp.where(deg == wave_grid, diagonal[None], 0.0)
        return (deg, first, second, lead, lag, offset)

    def compose(carry, step):
        g00, g01, g10, g11, h0, h1 = carry
        _, _, _, lead, lag, offset = factors(step)
        n00 = lead * g00 + lag * g10
        n01 = lead * g01 + lag * g11
        n0 = lead * h0 + lag * h1 + offset
        return ((n00, n01, g00, g01, n0, h0), None)

    ones = jnp.ones((blocks, count, LATITUDE_ROWS), jnp.float32)
    zeros = jnp.zeros((blocks, count, LATITUDE_ROWS), jnp.float32)
    maps, _ = lax.scan(
        compose, (ones, zeros, zeros, ones, zeros, zeros), jnp.arange(piece, dtype=jnp.int32)
    )

    def chain(carry, block_map):
        s0, s1 = carry
        g00, g01, g10, g11, h0, h1 = block_map
        return ((g00 * s0 + g01 * s1 + h0, g10 * s0 + g11 * s1 + h1), (s0, s1))

    flat = jnp.zeros((count, LATITUDE_ROWS), jnp.float32)
    _, starts = lax.scan(chain, (flat, flat), maps)

    def advance(carry, step):
        prev, before = carry
        deg, first, second, _, _, _ = factors(step)
        recur = first * (cos_grid * prev - second * before)
        fresh = jnp.where(deg < wave_grid, 0.0, jnp.where(deg == wave_grid, diagonal[None], recur))
        return ((fresh, prev), fresh * weight[None, None, :])

    _, table = lax.scan(advance, starts, jnp.arange(piece, dtype=jnp.int32))
    return jnp.transpose(table, (1, 0, 2, 3)).reshape(LMAX, count, LATITUDE_ROWS)


def apply_layer_norm(flat, gain):
    values = flat.astype(jnp.float32)
    mean_removed = values - jnp.mean(values, axis=-1, keepdims=True)
    standardized_input = mean_removed * lax.rsqrt(
        jnp.mean(mean_removed * mean_removed, axis=-1, keepdims=True) + 1e-05
    )
    return (standardized_input, (standardized_input * gain[None, :]).astype(jnp.bfloat16))


def slope(diff):
    return diff / jnp.sqrt(diff * diff + 0.01)


def per_device(embedding, target, gain, head_w):
    highest = lax.Precision.HIGHEST
    ensemble_member = embedding[0]
    lat_rows = ensemble_member.shape[0]
    grid_points = lat_rows * LONGITUDE_COLUMNS
    standardized_input, normalized_input = apply_layer_norm(
        ensemble_member.reshape(grid_points, EMBED_CHANNELS), gain
    )
    pred = lax.dot_general(
        head_w, normalized_input, (((0,), (1,)), ((), ())), preferred_element_type=jnp.float32
    )
    table = dft_table()
    pred_four = jnp.dot(
        pred.reshape(NVAR * lat_rows, LONGITUDE_COLUMNS),
        table,
        precision=highest,
        preferred_element_type=jnp.float32,
    )
    pred_four = pred_four.reshape(NVAR, lat_rows, 2 * MMAX)
    wave_count = MMAX // lax.axis_size("sp")
    basis = legendre_rows(lax.axis_index("sp") * wave_count, wave_count)

    def project(cols):
        four = cols.reshape(NVAR, LATITUDE_ROWS, wave_count, 2)
        return jnp.einsum("lmj,vjmp->vmpl", basis, four, precision=highest).reshape(
            NVAR, 2 * wave_count, LMAX
        )

    members = lax.axis_size("ens")
    true_four = jnp.dot(
        target.astype(jnp.float32).reshape(NVAR * lat_rows, LONGITUDE_COLUMNS),
        table,
        precision=highest,
        preferred_element_type=jnp.float32,
    )
    true_four = true_four.reshape(NVAR, lat_rows, 2 * MMAX)
    pred_cols, true_cols = (
        lax.all_to_all(pred_four, "sp", split_axis=2, concat_axis=1, tiled=True),
        lax.all_to_all(true_four, "sp", split_axis=2, concat_axis=1, tiled=True),
    )
    truth = project(true_cols)
    coef = project(pred_cols)
    pair = jnp.zeros_like(coef) + jnp.sum(
        slope(coef[None] - lax.all_gather(coef[None], "ens", axis=0, tiled=True)), axis=0
    )
    gcoef = (slope(coef - truth) / members - pair / (members * (members - 1))) / LMAX
    gfour = jnp.einsum(
        "lmj,vmpl->vjmp", basis, gcoef.reshape(NVAR, wave_count, 2, LMAX), precision=highest
    )
    gfour = gfour.reshape(NVAR, LATITUDE_ROWS, 2 * wave_count)
    grid_cols = lax.all_to_all(gfour, "sp", split_axis=1, concat_axis=2, tiled=True)
    gpred = jnp.dot(
        grid_cols.reshape(NVAR * lat_rows, 2 * MMAX),
        table.T,
        precision=highest,
        preferred_element_type=jnp.float32,
    )
    gpred = gpred.astype(jnp.bfloat16).reshape(NVAR, grid_points)
    dweight = lax.dot_general(
        normalized_input, gpred, (((0,), (1,)), ((), ())), preferred_element_type=jnp.float32
    )
    normalized_gradient = lax.dot_general(
        gpred, head_w, (((0,), (1,)), ((), ())), preferred_element_type=jnp.float32
    )
    gain_gradient = jnp.sum(normalized_gradient * standardized_input, axis=0)
    grad_head_w, grad_gain = lax.psum((dweight, gain_gradient), ("ens", "sp"))
    return (grad_head_w, grad_gain)


def solution(mesh):
    in_specs = (P("ens", "sp", None, None), P(None, "sp", None), P(), P())
    out_specs = (P(), P())
    return jax.shard_map(
        per_device, mesh=mesh, in_specs=in_specs, out_specs=out_specs, check_vma=False
    )
```

profile of v0, /device:TPU:1, one launch (start us, length us, event | category | flops | bytes accessed | tf_op | source)
XLA Modules:
  0.0 638.6 jit_solution(9708628167679571385)
XLA Ops:
  7.2 1.7 convert_reduce_fusion
  13.9 1.9 fusion.32
  18.3 2.6 copy.55
  20.9 3.0 reshape.813
  23.9 11.0 %all-to-all-start = ((f32[32,1,1728]{2,1,0:T(1,128)}), f32[32,1,1728]{2,1,0:T(1,128)}, u32[]{:S(2)}, u32[]{:S(2)}) async-start(f32[32,1,1728]{2,1,0:T(1,128)} %reshape.813), calls=%async_computation | async-start | bytes 458752 | tf_op jit(solution)/shard_map/all_to_all | solution.py:161
  45.1 98.3 %while.64 = (s32[]{:T(128)}, f32[16,6,192]{2,1,0:T(8,128)}, f32[16,6,192]{2,1,0:T(8,128)}, f32[16,6,192]{2,1,0:T(8,128)}, f32[16,6,192]{2,1,0:T(8,128)}, /*index...) while((s32[]{:T(128)}, f32[16,6,192]{2,1,0:T(8,128)}, ...), condition=%wide.region_5.6_spmd.clone.clone.clone, body=%wide.region_4.5_spmd.clone.clone.clone.sunk | while | flops 299297 | bytes 899223 | solution.py:88
  51.0 2.1 select_add_fusion.2
  59.1 2.2 select_add_fusion.2
  67.3 2.2 select_add_fusion.2
  75.5 2.2 select_add_fusion.2
  83.7 2.2 select_add_fusion.2
  91.9 2.2 select_add_fusion.2
  100.1 2.2 select_add_fusion.2
  108.3 2.2 select_add_fusion.2
  116.5 2.2 select_add_fusion.2
  124.7 2.2 select_add_fusion.2
  132.9 2.2 select_add_fusion.2
  141.2 2.2 select_add_fusion.2
  144.7 43.1 %while.62 = (s32[]{:T(128)}, f32[6,192]{1,0:T(8,128)}, f32[6,192]{1,0:T(8,128)}, f32[16,6,192]{2,1,0:T(8,128)}, f32[16,6,192]{2,1,0:T(8,128)}, /*index=5*/f32[16...) while((s32[]{:T(128)}, f32[6,192]{1,0:T(8,128)}, ...), condition=%wide.region_7.8_spmd.clone, body=%wide.region_6.7_spmd.clone.sunk | while | flops 13827 | bytes 79500 | solution.py:98
  188.3 126.4 %while.63 = (s32[]{:T(128)}, f32[16,6,192]{2,1,0:T(8,128)}, f32[16,6,192]{2,1,0:T(8,128)}, f32[12,16,6,192]{3,2,1,0:T(8,128)}, s32[12]{0:T(128)}, /*index=5*/s32...) while((s32[]{:T(128)}, f32[16,6,192]{2,1,0:T(8,128)}, ...), condition=%wide.region_9.10_spmd.clone.clone, body=%wide.region_8.9_spmd.clone.clone.sunk | while | flops 133792 | bytes 795413 | solution.py:107
  194.9 1.8 bitcast_dynamic-update-slice_fusion.6
  205.4 1.8 bitcast_dynamic-update-slice_fusion.6
  215.9 1.8 bitcast_dynamic-update-slice_fusion.6
  226.5 1.8 bitcast_dynamic-update-slice_fusion.6
  237.0 1.8 bitcast_dynamic-update-slice_fusion.6
  247.5 1.8 bitcast_dynamic-update-slice_fusion.6
  258.1 1.8 bitcast_dynamic-update-slice_fusion.6
  268.6 1.8 bitcast_dynamic-update-slice_fusion.6
  279.1 1.8 bitcast_dynamic-update-slice_fusion.6
  289.7 1.8 bitcast_dynamic-update-slice_fusion.6
  300.2 1.8 bitcast_dynamic-update-slice_fusion.6
  310.8 1.8 bitcast_dynamic-update-slice_fusion.6
  314.7 3.3 copy.58
  318.0 2.5 reshape.810
  321.1 2.8 reduce.4
  323.9 3.0 reshape.814
  326.8 2.7 copy.57
  329.6 2.4 reshape.798
  332.0 4.3 fusion.39
  339.5 2.2 convolution_bitcast_fusion
  341.7 1.7 reshape.803
  343.4 2.6 copy.61
  346.0 3.0 reshape.815
  349.0 28.0 %all_to_all.45 = f32[32,1,1728]{2,1,0:T(1,128)} all-to-all(f32[32,1,1728]{2,1,0:T(1,128)} %reshape.815), channel_id=1, replica_groups=mesh['ens'=16,'sp'=32] {'sp'}, dimensions={0} | all-to-all | bytes 442368 | tf_op jit(solution)/shard_map/all_to_all | solution.py:162
  377.0 2.8 reduce.5
  379.9 2.9 reshape.816
  382.8 2.7 copy.63
  385.5 2.5 reshape.804
  388.0 4.4 fusion.45
  392.4 93.9 %all-gather.2.cloned.1.call-done = f32[16,24,12,192]{3,1,2,0:T(8,128)} async-done(((f32[1,24,12,192]{3,1,2,0:T(8,128)}), f32[16,24,12,192]{3,1,2,0:T(8,128)}) %all-gather.2.cloned.1.call-update) | async-done | bytes 3538960 | tf_op jit(solution)/shard_map/all_gather | solution.py:167
  486.3 3.5 multiply_reduce_fusion
  489.8 1.6 fusion.35
  491.5 2.8 copy.65
  494.3 3.0 reshape.817
  497.3 6.0 all-to-all-start.2
  503.3 2.4 multiply_convert_fusion.1
  505.7 8.3 %all-to-all-done.2 = f32[32,1,1728]{2,1,0:T(1,128)} async-done(((f32[32,1,1728]{2,1,0:T(1,128)}), f32[32,1,1728]{2,1,0:T(1,128)}, u32[]{:S(2)}, u32[]{:S(2)}) %all-to-all-start.2) | async-done | bytes 221216 | tf_op jit(solution)/shard_map/all_to_all | solution.py:174
  513.9 2.1 reduce.6
  516.1 2.0 reshape.818
  518.1 4.4 copy.67
  522.5 3.3 reshape.806
  527.1 1.7 reshape.807
  528.8 1.7 fusion.33
  530.8 101.0 %all-reduce.1 = (f32[256,24]{0,1:T(8,128)}, f32[256]{0:T(256)}) all-reduce(f32[256,24]{0,1:T(8,128)S(1)} %fusion.72, f32[256]{0:T(256)S(1)} %fusion.33), channel_id=1, replica_groups=mesh['ens'=16,'sp'=32] {'ens','sp'}, use_global_device_ids=true, to_apply=%region_11.12 | all-reduce | flops 6400 | bytes 51200 | tf_op jit(solution)/shard_map/psum | solution.py:189
  (400 shorter events, 243.4 us)
Async XLA Ops:
  7.2 8.7 %copy-start = (bf16[256,24]{0,1:T(8,128)(2,1)S(1)}, bf16[256,24]{0,1:T(8,128)(2,1)}, u32[]{:S(2)}) copy-start(bf16[256,24]{0,1:T(8,128)(2,1)} %param.13) | copy-start | bytes 36868
  7.2 1.8 copy-start.1
  9.0 3.2 copy-start.8
  11.5 0.6 copy-start.9
  13.9 1.9 copy-start.10
  15.8 1.1 copy-start.3
  23.9 296.6 %all-to-all-start = ((f32[32,1,1728]{2,1,0:T(1,128)}), f32[32,1,1728]{2,1,0:T(1,128)}, u32[]{:S(2)}, u32[]{:S(2)}) async-start(f32[32,1,1728]{2,1,0:T(1,128)} %reshape.813), calls=%async_computation | async-start | bytes 458752 | tf_op jit(solution)/shard_map/all_to_all | solution.py:161
  35.0 451.3 %all-gather.2.cloned.1.call-start = ((), (), s32[]{:S(2)}) async-start(), calls=%async_computation.3 | async-start | bytes 5013504 | tf_op jit(solution)/shard_map/all_gather | solution.py:167
  486.3 3.6 copy-start.2
  486.3 3.6 copy-start.6
  494.3 9.0 %copy-start.11 = (f32[256]{0:T(256)S(1)}, f32[256]{0:T(256)}, u32[]{:S(2)}) copy-start(f32[256]{0:T(256)} %param.12) | copy-start | bytes 3076
  497.3 16.6 %all-to-all-start.2 = ((f32[32,1,1728]{2,1,0:T(1,128)}), f32[32,1,1728]{2,1,0:T(1,128)}, u32[]{:S(2)}, u32[]{:S(2)}) async-start(f32[32,1,1728]{2,1,0:T(1,128)} %reshape.817), calls=%async_computation.2 | async-start | bytes 458752 | tf_op jit(solution)/shard_map/all_to_all | solution.py:174
  522.5 3.3 copy-start.4
  527.1 3.4 copy-start.5
  528.8 1.7 copy-start.7
Sparse Core Ops, SparseCore 0:
  336.5 149.7 all-gather.1
where the time goes:
time: 644 us; the launch traced here: 639 us
  other arithmetic  211 us (33%)
  local copies, waits for them, and re-layouts  146 us (23%)
  blocking collectives  129 us (20%)
  waiting for transfers between devices  102 us (16%)
  matrix products  17.7 us (3%)
  starting transfers between devices  17.2 us (3%)
  between operations  14.3 us (2%)
    psum x1, blocking collectives, per_device(): grad_head_w, grad_gain = lax.psum((dweight, gain_gradient), ('ens', 'sp'))  101 us
    all_gather x1, waiting for transfers between devices, per_device(): lax.all_gather(coef[None], 'ens', axis=0, tiled=True)  93.9 us
    dynamic_slice x24, local copies, waits for them, and re-layouts, legendre_rows(): lax.scan(compose, (ones, zeros, zeros, ones, zeros, zeros), jnp.arange(pi...  29.7 us
    all_to_all x1, blocking collectives, per_device(): lax.all_to_all(true_four, 'sp', split_axis=2, concat_axis=1, tiled=True)  28 us
    add x12, other arithmetic, compose(): n0 = lead * h0 + lag * h1 + offset  26.8 us
    while x24, local copies, waits for them, and re-layouts  26.6 us
    exp x24, other arithmetic, legendre_rows(): jnp.exp(0.5 * jnp.log((2.0 * waves + 1.0) / (4.0 * math.pi)) + 0.5 * part...  25.4 us
    add x16, other arithmetic, chain(): return ((g00 * s0 + g01 * s1 + h0, g10 * s0 + g11 * s1 + h1), (s0, s1))  22.7 us
  transfers between devices with their start and end apart: 3, of which 2 were waited for; matrix products, arithmetic and copies ran while one was open for 49% of the time, Pallas kernels for 0%

commit v1 on v0

v1 whole, which is shorter than its diff:
```python
import functools
import math

import jax
import jax.numpy as jnp
import ml_dtypes
import numpy as np
from jax import lax
from jax.experimental import pallas as pl
from jax.experimental.pallas import tpu as pltpu
from jax.sharding import PartitionSpec as P

EMBED = 256
NVAR = 24
ROWS = 192
COLS = 384
MMAX = 192
LMAX = 192
MEMBERS = 16
SP = 32
LOCAL_ROWS = ROWS // SP
POINTS = LOCAL_ROWS * COLS
PAIRS = 3
MESH = pl.DeviceIdType.MESH
F32 = jnp.float32
BF16 = jnp.bfloat16


def split_np(x):
    hi = x.astype(np.float32).astype(ml_dtypes.bfloat16)
    lo = (x - hi.astype(np.float64)).astype(np.float32).astype(ml_dtypes.bfloat16)
    return np.stack([hi, lo])


def pair_waves():
    q = (np.arange(PAIRS)[:, None] * SP + np.arange(SP)[None, :])
    return np.stack([q, MMAX - 1 - q])


def dft_tables():
    waves = pair_waves().reshape(2, PAIRS * SP)
    phase = (waves[:, :, None] * np.arange(COLS)[None, None, :]) % COLS
    angle = phase * (2.0 * math.pi / COLS)
    factor = 2.0 * math.pi / COLS
    table = np.stack([np.cos(angle), -np.sin(angle)], axis=1) * factor
    forward = table.reshape(4 * PAIRS * SP, COLS)
    back = np.zeros((4, 128, COLS))
    back[:, : PAIRS * SP] = table.reshape(4, PAIRS * SP, COLS)
    return split_np(forward), split_np(back.reshape(512, COLS))


def legendre_basis():
    theta = math.pi * (np.arange(ROWS) + 0.5) / ROWS
    x, sine = np.cos(theta), np.sin(theta)
    m = np.arange(MMAX, dtype=np.float64)[:, None]
    q = np.arange(1, MMAX, dtype=np.float64)
    running = np.concatenate([[0.0], np.cumsum(np.log((2 * q - 1) / (2 * q)))])[:, None]
    diagonal = np.exp(
        0.5 * np.log((2 * m + 1) / (4 * math.pi)) + 0.5 * running + m * np.log(sine)[None, :]
    )
    weight = math.pi / ROWS * sine * math.sqrt(ROWS * COLS / (4 * math.pi))
    out = np.zeros((LMAX, MMAX, ROWS))
    prev, before = np.zeros((MMAX, ROWS)), np.zeros((MMAX, ROWS))
    for l in range(LMAX):
        a = np.sqrt((4.0 * l * l - 1.0) / np.maximum(l * l - m * m, 1.0)) if l else np.zeros_like(m)
        b = np.sqrt(
            np.maximum((l - 1.0) ** 2 - m * m, 0.0) / np.maximum(4.0 * (l - 1.0) ** 2 - 1.0, 1.0)
        )
        fresh = np.where(l < m, 0.0, np.where(l == m, diagonal, a * (x[None] * prev - b * before)))
        out[l] = fresh * weight[None]
        prev, before = fresh, prev
    return out


def legendre_table():
    basis = legendre_basis()
    table = np.zeros((SP, PAIRS, 256, SP, 8))
    for s in range(SP):
        for i in range(PAIRS):
            q = SP * i + s
            first = basis[q:, q].reshape(-1, SP, LOCAL_ROWS)
            second = basis[MMAX - 1 - q :, MMAX - 1 - q].reshape(-1, SP, LOCAL_ROWS)
            table[s, i, : MMAX - q, :, :LOCAL_ROWS] = first
            table[s, i, MMAX - q : MMAX + 1, :, :LOCAL_ROWS] = second
    both = split_np(table.reshape(SP, PAIRS, 256, 256))
    return np.ascontiguousarray(np.moveaxis(both, 0, 2))


def split(x):
    hi = x.astype(BF16)
    return hi, (x - hi.astype(F32)).astype(BF16)


def dot(a, b):
    return jnp.dot(a, b, preferred_element_type=F32)


def dot_t(a, b):
    return lax.dot_general(a, b, (((1,), (1,)), ((), ())), preferred_element_type=F32)


def three(product, a, b):
    return product(a[0], b[0]) + (product(a[1], b[0]) + product(a[0], b[1]))


def slope(diff):
    return diff * lax.rsqrt(diff * diff + 0.01)


def standardize(values):
    centred = values - jnp.mean(values, axis=-1, keepdims=True)
    return centred * lax.rsqrt(jnp.mean(centred * centred, axis=-1, keepdims=True) + 1e-05)


def kernel(
    emb_hbm, target_ref, gain_ref, head_ref, fwd_ref, back_ref, leg_hbm,
    out_ref,
    emb_ref, leg_ref, feat_ref, target_rows, grid_ref, waves_ref,
    tsend, trecv, psend, precv, csend, crecv, ctruth, gsend, grecv, bsend, brecv,
    rsend, rrecv, esend, erecv,
    load_sem, send_sem, recv_sem,
):
    e = lax.axis_index("ens")
    s = lax.axis_index("sp")
    barrier = pltpu.get_barrier_semaphore()

    def greet_sp(d, carry):
        pl.semaphore_signal(barrier, inc=1, device_id=(e, (s + d) % SP), device_id_type=MESH)
        return carry

    def greet_ens(d, carry):
        pl.semaphore_signal(barrier, inc=1, device_id=((e + d) % MEMBERS, s), device_id_type=MESH)
        return carry

    emb_copy = pltpu.make_async_copy(emb_hbm, emb_ref, load_sem.at[0])
    emb_copy.start()
    leg_copy = pltpu.make_async_copy(leg_hbm.at[s], leg_ref, load_sem.at[1])
    leg_copy.start()
    lax.fori_loop(1, SP, greet_sp, 0)
    lax.fori_loop(1, MEMBERS, greet_ens, 0)

    lane = lax.broadcasted_iota(jnp.int32, (1, 128), 1)
    wide_lane = lax.broadcasted_iota(jnp.int32, (1, 256), 1)

    def waves_to_blocks(target_block):
        field = split(grid_ref[...])
        table = (fwd_ref[0], fwd_ref[1])
        waves_ref[...] = three(dot_t, table, field)
        for row in range(LOCAL_ROWS):
            group, start = (0, 24 * row) if row < 5 else (1, 0)
            parts = [
                pltpu.roll(
                    waves_ref[96 * hp : 96 * hp + 96, 128 * group : 128 * group + 128],
                    (24 * hp - start) % 128, 1,
                )
                for hp in range(4)
            ]
            block = jnp.where(
                lane < 48,
                jnp.where(lane < 24, parts[0], parts[1]),
                jnp.where(lane < 72, parts[2], parts[3]),
            )
            for i in range(PAIRS):
                target_block[i, pl.ds(row, SP, stride=8), :] = block[SP * i : SP * i + SP]

    def exchange_sp(source, dest, at):
        def send(d, carry):
            to = (s + d) % SP
            pltpu.make_async_remote_copy(
                src_ref=source.at[:, pl.ds(pl.multiple_of(8 * to, 8), 8), :],
                dst_ref=dest.at[:, pl.ds(pl.multiple_of(8 * s, 8), 8), :],
                send_sem=send_sem.at[at], recv_sem=recv_sem.at[at],
                device_id=(e, to), device_id_type=MESH,
            ).start()
            return carry

        lax.fori_loop(1, SP, send, 0)
        mine = pl.ds(pl.multiple_of(8 * s, 8), 8)
        dest[:, mine, :] = source[:, mine, :]

    def exchange_ens(source, dest, at):
        def send(d, carry):
            to = (e + d) % MEMBERS
            pltpu.make_async_remote_copy(
                src_ref=source.at[to], dst_ref=dest.at[e],
                send_sem=send_sem.at[at], recv_sem=recv_sem.at[at],
                device_id=(to, s), device_id_type=MESH,
            ).start()
            return carry

        lax.fori_loop(1, MEMBERS, send, 0)
        dest[e] = source[e]

    def settle(piece, sem):
        pltpu.make_async_copy(piece, piece, sem).wait()

    def sp_piece(ref):
        return ref.at[:, pl.ds(0, 8 * (SP - 1)), :]

    def ens_piece(ref):
        return ref.at[pl.ds(0, MEMBERS - 1)]

    pad = jnp.zeros((PAIRS, 256, 128), F32)
    tsend[...] = pad
    psend[...] = pad
    grid_ref[...] = jnp.zeros((256, COLS), F32)
    for v in range(NVAR):
        for c in range(3):
            target_rows[c, 8 * v : 8 * v + LOCAL_ROWS, :] = target_ref[
                v, :, 128 * c : 128 * c + 128
            ].astype(F32)
    for row in range(LOCAL_ROWS):
        at = 24 * row if row < 5 else 128
        for c in range(3):
            grid_ref[at : at + 24, 128 * c : 128 * c + 128] = target_rows[
                c, pl.ds(row, NVAR, stride=8), :
            ]
    waves_to_blocks(tsend)
    pl.semaphore_wait(barrier, SP - 1 + MEMBERS - 1)
    exchange_sp(tsend, trecv, 0)

    emb_copy.wait()
    head_t = head_ref[...].astype(F32).T
    head_t16 = head_t.astype(BF16)
    gain = gain_ref[...]
    step = 64

    def norm_chunk(at, carry):
        rows = pl.ds(pl.multiple_of(at * step, step), step)
        xhat = standardize(emb_ref[rows, :].astype(F32))
        feat_ref[rows, 0:256] = (xhat * gain).astype(BF16)
        return carry

    lax.fori_loop(0, POINTS // step, norm_chunk, 0)
    for row in range(LOCAL_ROWS):
        at = 24 * row if row < 5 else 128
        grid_ref[at : at + 24, :] = dot_t(head_t16, feat_ref[COLS * row : COLS * row + COLS, 0:256])
    waves_to_blocks(psend)
    exchange_sp(psend, precv, 1)

    def xhat_chunk(at, carry):
        rows = pl.ds(pl.multiple_of(at * step, step), step)
        hi, lo = split(standardize(emb_ref[rows, :].astype(F32)))
        feat_ref[rows, 256:512] = hi
        feat_ref[rows, 512:768] = lo
        return carry

    lax.fori_loop(0, POINTS // step, xhat_chunk, 0)
    leg_copy.wait()

    def to_coefficients(received, slices):
        tails = []
        for i in range(PAIRS):
            basis = (leg_ref[i, 0], leg_ref[i, 1])
            terms = three(dot, basis, split(received[i])).T
            edge = MMAX - (SP * i + s)
            packed = jnp.where(wide_lane < edge, terms[0:48], terms[48:96])
            for b in range(3):
                slices[3 * i + b] = packed[16 * b : 16 * b + 16, 0:128]
            tails.append(packed[:, 128:256])
        group3 = jnp.where(lane < 65, tails[0], pltpu.roll(tails[1], 65, 1))
        group4 = jnp.where(
            lane < 65, tails[2], jnp.where(lane < 67, pltpu.roll(tails[1], 2, 1), 0.0)
        )
        for b in range(3):
            slices[9 + b] = group3[16 * b : 16 * b + 16]
            slices[12 + b] = group4[16 * b : 16 * b + 16]
        slices[15] = jnp.zeros((16, 128), F32)

    settle(sp_piece(trecv), recv_sem.at[0])
    to_coefficients(trecv, ctruth)
    settle(sp_piece(precv), recv_sem.at[1])
    to_coefficients(precv, csend)
    exchange_ens(csend, crecv, 2)
    truth = ctruth[e]
    settle(ens_piece(crecv), recv_sem.at[2])

    members = crecv[...]

    def turned(x, by):
        by = by % MEMBERS
        return jnp.concatenate([x[MEMBERS - by :], x[: MEMBERS - by]], axis=0)

    pair = slope(members - turned(members, 8))
    for by in range(1, 8):
        term = slope(members - turned(members, by))
        pair = pair + (term - turned(term, -by))
    gsend[...] = slope(members - truth[None]) * (1.0 / (MEMBERS * LMAX)) - pair * (
        1.0 / (MEMBERS * (MEMBERS - 1) * LMAX)
    )
    exchange_ens(gsend, grecv, 3)
    settle(ens_piece(grecv), recv_sem.at[3])

    groups = [
        jnp.concatenate([grecv[3 * c + b] for b in range(3)], axis=0) for c in range(5)
    ]
    tails = [
        jnp.where(lane < 65, groups[3], 0.0),
        jnp.where(
            lane < 63,
            pltpu.roll(groups[3], 63, 1),
            jnp.where(lane < 65, pltpu.roll(groups[4], 126, 1), 0.0),
        ),
        jnp.where(lane < 65, groups[4], 0.0),
    ]
    for i in range(PAIRS):
        packed = jnp.concatenate([groups[i], tails[i]], axis=1)
        edge = MMAX - (SP * i + s)
        both = jnp.concatenate(
            [
                jnp.where(wide_lane < edge, packed, 0.0),
                jnp.where(wide_lane < edge, 0.0, packed),
                jnp.zeros((32, 256), F32),
            ],
            axis=0,
        )
        basis = (leg_ref[i, 0], leg_ref[i, 1])
        bsend[i] = three(dot, split(both), basis).T
    exchange_sp(bsend, brecv, 4)
    settle(sp_piece(brecv), recv_sem.at[4])

    pieces = []
    for row in range(LOCAL_ROWS):
        block = jnp.concatenate(
            [brecv[i, pl.ds(row, SP, stride=8), :] for i in range(PAIRS)]
            + [jnp.zeros((32, 128), F32)],
            axis=0,
        ).T
        pieces.append(
            jnp.concatenate([block[24 * hp : 24 * hp + 24] for hp in range(4)], axis=1)
        )
    waves = jnp.concatenate(pieces, axis=0)
    table = (back_ref[0], back_ref[1])
    gpred = three(dot, split(waves), table)
    flat = jnp.concatenate(
        [gpred[24 * row : 24 * row + 24] for row in range(LOCAL_ROWS)], axis=1
    ).astype(BF16)
    grads = dot(flat, feat_ref[...])
    gain_grad = jnp.sum(
        (grads[:, 256:512] + grads[:, 512:768]) * head_t, axis=0, keepdims=True
    )
    for v in range(NVAR):
        rsend[v] = grads[v : v + 1, 0:256]
    rsend[NVAR] = gain_grad
    for r in range(NVAR + 1, SP):
        rsend[r] = jnp.zeros((1, 256), F32)

    def scatter(d, carry):
        to = (s + d) % SP
        pltpu.make_async_remote_copy(
            src_ref=rsend.at[to], dst_ref=rrecv.at[s],
            send_sem=send_sem.at[5], recv_sem=recv_sem.at[5],
            device_id=(e, to), device_id_type=MESH,
        ).start()
        return carry

    lax.fori_loop(1, SP, scatter, 0)
    rrecv[s] = rsend[s]
    settle(rrecv.at[pl.ds(0, SP - 1)], recv_sem.at[5])
    total = rrecv[0]
    for r in range(1, SP):
        total = total + rrecv[r]
    esend[...] = total

    def spread(d, carry):
        to = (e + d) % MEMBERS
        pltpu.make_async_remote_copy(
            src_ref=esend, dst_ref=erecv.at[e],
            send_sem=send_sem.at[6], recv_sem=recv_sem.at[6],
            device_id=(to, s), device_id_type=MESH,
        ).start()
        return carry

    lax.fori_loop(1, MEMBERS, spread, 0)
    erecv[e] = total
    settle(erecv.at[pl.ds(0, MEMBERS - 1)], recv_sem.at[6])
    total = erecv[0]
    for r in range(1, MEMBERS):
        total = total + erecv[r]
    out_ref[s] = total

    def gather(d, carry):
        to = (s + d) % SP
        pltpu.make_async_remote_copy(
            src_ref=out_ref.at[s], dst_ref=out_ref.at[s],
            send_sem=send_sem.at[7], recv_sem=recv_sem.at[7],
            device_id=(e, to), device_id_type=MESH,
        ).start()
        return carry

    lax.fori_loop(1, SP, gather, 0)
    settle(out_ref.at[pl.ds(0, SP - 1)], recv_sem.at[7])

    settle(sp_piece(tsend), send_sem.at[0])
    settle(sp_piece(psend), send_sem.at[1])
    settle(ens_piece(csend), send_sem.at[2])
    settle(ens_piece(gsend), send_sem.at[3])
    settle(sp_piece(bsend), send_sem.at[4])
    settle(rsend.at[pl.ds(0, SP - 1)], send_sem.at[5])
    settle(erecv.at[pl.ds(0, MEMBERS - 1)], send_sem.at[6])
    settle(out_ref.at[pl.ds(0, SP - 1)], send_sem.at[7])


def per_device(forward, back, legendre, embedding, target, gain, head_w):
    vmem = pl.BlockSpec(memory_space=pltpu.VMEM)
    anywhere = pl.BlockSpec(memory_space=pl.ANY)
    block = (PAIRS, 256, 128)
    ens_block = (MEMBERS, 16, 128)
    sums = pl.pallas_call(
        kernel,
        out_shape=jax.ShapeDtypeStruct((SP, 1, 256), F32),
        in_specs=[anywhere, vmem, vmem, vmem, vmem, vmem, anywhere],
        out_specs=vmem,
        scratch_shapes=[
            pltpu.VMEM((POINTS, EMBED), BF16),
            pltpu.VMEM((PAIRS, 2, 256, 256), BF16),
            pltpu.VMEM((POINTS, 3 * EMBED), BF16),
            pltpu.VMEM((3, 8 * NVAR, 128), F32),
            pltpu.VMEM((256, COLS), F32),
            pltpu.VMEM((384, 256), F32),
            pltpu.VMEM(block, F32),
            pltpu.VMEM(block, F32),
            pltpu.VMEM(block, F32),
            pltpu.VMEM(block, F32),
            pltpu.VMEM(ens_block, F32),
            pltpu.VMEM(ens_block, F32),
            pltpu.VMEM(ens_block, F32),
            pltpu.VMEM(ens_block, F32),
            pltpu.VMEM(ens_block, F32),
            pltpu.VMEM(block, F32),
            pltpu.VMEM(block, F32),
            pltpu.VMEM((SP, 1, 256), F32),
            pltpu.VMEM((SP, 1, 256), F32),
            pltpu.VMEM((1, 256), F32),
            pltpu.VMEM((MEMBERS, 1, 256), F32),
            pltpu.SemaphoreType.DMA((2,)),
            pltpu.SemaphoreType.DMA((8,)),
            pltpu.SemaphoreType.DMA((8,)),
        ],
        compiler_params=pltpu.CompilerParams(
            collective_id=0, has_side_effects=True, vmem_limit_bytes=40 * 1024 * 1024
        ),
        name="crps",
    )(
        embedding.reshape(POINTS, EMBED), target, gain.reshape(1, EMBED), head_w,
        forward, back, legendre,
    )
    return sums[:NVAR, 0].T, sums[NVAR, 0]


def solution(mesh):
    forward, back = dft_tables()
    legendre = legendre_table()
    in_specs = (P("ens", "sp", None, None), P(None, "sp", None), P(), P())

    def run(*args):
        return jax.shard_map(
            functools.partial(
                per_device, jnp.asarray(forward), jnp.asarray(back), jnp.asarray(legendre)
            ),
            mesh=mesh, in_specs=in_specs, out_specs=(P(), P()), check_vma=False,
        )(*args)

    return run
```

time: 644 us -> 95.5 us (0.15)
  other arithmetic: 211 us -> 0 us
  local copies, waits for them, and re-layouts: 146 us -> 7.07 us
  blocking collectives: 129 us -> 0 us
  waiting for transfers between devices: 102 us -> 0 us
  Pallas kernels: 0 us -> 87.5 us
  matrix products: 17.7 us -> 0 us
  starting transfers between devices: 17.2 us -> 0 us
  between operations: 14.3 us -> 0.65 us
    psum x1 -> x0, blocking collectives: 101 us -> none  [per_device(): grad_head_w, grad_gain = lax.psum((dweight, gain_gradient), ('ens', 'sp'))]
    all_gather x1 -> x0, waiting for transfers between devices: 93.9 us -> none  [per_device(): lax.all_gather(coef[None], 'ens', axis=0, tiled=True)]
    pallas_call x0 -> x1, Pallas kernels: none -> 87.5 us  [per_device(): pl.pallas_call(kernel, out_shape=jax.ShapeDtypeStruct((SP, 1, 256), F32),...]
    add x29 -> x0, other arithmetic: 50.1 us -> none  [the longest x12 26.8 us: compose(): n0 = lead * h0 + lag * h1 + offset]
    dynamic_update_slice x28 -> x0, other arithmetic: 41.8 us -> none  [the longest x12 21.4 us: legendre_rows(): _, table = lax.scan(advance, starts, jnp.arange(piece, dtype=jnp.int32))]
    dynamic_slice x24 -> x0, local copies, waits for them, and re-layouts: 29.7 us -> none  [legendre_rows(): lax.scan(compose, (ones, zeros, zeros, ones, zeros, zeros), jnp.arange(pi...]
    all_to_all x1 -> x0, blocking collectives: 28 us -> none  [per_device(): lax.all_to_all(true_four, 'sp', split_axis=2, concat_axis=1, tiled=True)]
    while x24 -> x0, local copies, waits for them, and re-layouts: 26.6 us -> none
  transfers between devices with their start and end apart: 3 -> 0, of which waited for: 2 -> 0; matrix products, arithmetic and copies ran while one was open for 49% -> 0% of each run, Pallas kernels for 0% -> 0%
where the time goes in v1:
time: 95.5 us; the launch traced here: 95.2 us
  Pallas kernels  87.5 us (92%)
  local copies, waits for them, and re-layouts  7.07 us (7%)
    pallas_call x1, Pallas kernels, per_device(): pl.pallas_call(kernel, out_shape=jax.ShapeDtypeStruct((SP, 1, 256), F32),...  87.5 us
    unnamed x11, local copies, waits for them, and re-layouts  6.5 us

profile of v1, /device:TPU:1, one launch (start us, length us, event | category | flops | bytes accessed | tf_op | source)
XLA Modules:
  0.0 95.2 jit_solution(15072396710745443203)
XLA Ops:
  0.6 0.8 copy.10.head_ref
  1.5 0.9 copy.9.target_ref
  2.4 0.0 copy-start
  2.4 1.3 %copy-done = bf16[1,6,384,256]{3,2,1,0:T(8,128)(2,1)S(1)} copy-done((bf16[1,6,384,256]{3,2,1,0:T(8,128)(2,1)S(1)}, bf16[1,6,384,256]{3,2,1,0:T(8,128)(2,1)}, u32[]{:S(2)}) %copy-start) | copy-done | bytes 1179672
  3.7 0.0 copy-start.1
  3.7 1.1 %copy-done.1 = bf16[2,512,384]{2,1,0:T(8,128)(2,1)S(1)} copy-done((bf16[2,512,384]{2,1,0:T(8,128)(2,1)S(1)}, bf16[2,512,384]{2,1,0:T(8,128)(2,1)}, u32[]{:S(2)}) %copy-start.1) | copy-done | bytes 786456
  4.8 0.0 copy-start.2
  4.8 1.1 %copy-done.2 = bf16[2,384,384]{2,1,0:T(8,128)(2,1)S(1)} copy-done((bf16[2,384,384]{2,1,0:T(8,128)(2,1)S(1)}, bf16[2,384,384]{2,1,0:T(8,128)(2,1)}, u32[]{:S(2)}) %copy-start.2) | copy-done | bytes 589848
  5.9 0.0 copy-start.3
  5.9 0.7 copy-done.3
  6.5 87.5 %crps.1 = f32[32,1,256]{2,1,0:T(1,128)S(1)} custom-call(bf16[2304,256]{1,0:T(8,128)(2,1)S(1)} %bitcast.8, bf16[24,6,384]{2,1,0:T(8,128)(2,1)S(1)} %copy.9.target_ref, f32[1,256]{1,0:T(1,128)S(1)} %bitcast.9, bf16[256,24]{1,0:T(8,128)(2,1)S(1)} %copy.10.head_ref, bf16[2,384,384]{2,1,0:T(8,128)(2,1)S(1)} %copy-done.2, bf16[2,512,384]{2,1,0:T(8,128)(2,1)S(1)} %copy-done.1, ...), custom_call_target="tpu_custom_call" | custom-call | tf_op jit(solution)/shard_map/crps/pallas_call | solution.py:409
  94.0 0.6 slice.7
  94.6 0.6 copy.13
  (1 shorter events, 0.0 us)
Async XLA Ops:
  2.4 1.3 %copy-start = (bf16[1,6,384,256]{3,2,1,0:T(8,128)(2,1)S(1)}, bf16[1,6,384,256]{3,2,1,0:T(8,128)(2,1)}, u32[]{:S(2)}) copy-start(bf16[1,6,384,256]{3,2,1,0:T(8,128)(2,1)} %param.7) | copy-start | bytes 3538948
  3.7 1.1 %copy-start.1 = (bf16[2,512,384]{2,1,0:T(8,128)(2,1)S(1)}, bf16[2,512,384]{2,1,0:T(8,128)(2,1)}, u32[]{:S(2)}) copy-start(bf16[2,512,384]{2,1,0:T(8,128)(2,1)} %constant.7.clone.back_ref) | copy-start | bytes 2359300
  4.8 1.1 %copy-start.2 = (bf16[2,384,384]{2,1,0:T(8,128)(2,1)S(1)}, bf16[2,384,384]{2,1,0:T(8,128)(2,1)}, u32[]{:S(2)}) copy-start(bf16[2,384,384]{2,1,0:T(8,128)(2,1)} %constant.6.clone.fwd_ref) | copy-start | bytes 1769476
  5.9 0.7 copy-start.3

commit v2 on v1

v2 whole, which is shorter than its diff:
```python
import functools
import math

import jax
import jax.numpy as jnp
import ml_dtypes
import numpy as np
from jax import lax
from jax.experimental import pallas as pl
from jax.experimental.pallas import tpu as pltpu
from jax.sharding import PartitionSpec as P

EMBED = 256
NVAR = 24
ROWS = 192
COLS = 384
MMAX = 192
LMAX = 192
MEMBERS = 16
SP = 32
LOCAL_ROWS = ROWS // SP
POINTS = LOCAL_ROWS * COLS
PAIRS = 3
STEP = 384
MESH = pl.DeviceIdType.MESH
F32 = jnp.float32
BF16 = jnp.bfloat16


def split_np(x):
    hi = x.astype(np.float32).astype(ml_dtypes.bfloat16)
    lo = (x - hi.astype(np.float64)).astype(np.float32).astype(ml_dtypes.bfloat16)
    return np.stack([hi, lo])


def pair_waves():
    q = (np.arange(PAIRS)[:, None] * SP + np.arange(SP)[None, :])
    return np.stack([q, MMAX - 1 - q])


def dft_tables():
    waves = pair_waves().reshape(2, PAIRS * SP)
    phase = (waves[:, :, None] * np.arange(COLS)[None, None, :]) % COLS
    angle = phase * (2.0 * math.pi / COLS)
    factor = 2.0 * math.pi / COLS
    table = np.stack([np.cos(angle), -np.sin(angle)], axis=1) * factor
    forward = table.reshape(4 * PAIRS * SP, COLS)
    back = np.zeros((4, 128, COLS))
    back[:, : PAIRS * SP] = table.reshape(4, PAIRS * SP, COLS)
    return split_np(forward), split_np(back.reshape(512, COLS))


def legendre_basis():
    theta = math.pi * (np.arange(ROWS) + 0.5) / ROWS
    x, sine = np.cos(theta), np.sin(theta)
    m = np.arange(MMAX, dtype=np.float64)[:, None]
    q = np.arange(1, MMAX, dtype=np.float64)
    running = np.concatenate([[0.0], np.cumsum(np.log((2 * q - 1) / (2 * q)))])[:, None]
    diagonal = np.exp(
        0.5 * np.log((2 * m + 1) / (4 * math.pi)) + 0.5 * running + m * np.log(sine)[None, :]
    )
    weight = math.pi / ROWS * sine * math.sqrt(ROWS * COLS / (4 * math.pi))
    out = np.zeros((LMAX, MMAX, ROWS))
    prev, before = np.zeros((MMAX, ROWS)), np.zeros((MMAX, ROWS))
    for l in range(LMAX):
        a = np.sqrt((4.0 * l * l - 1.0) / np.maximum(l * l - m * m, 1.0)) if l else np.zeros_like(m)
        b = np.sqrt(
            np.maximum((l - 1.0) ** 2 - m * m, 0.0) / np.maximum(4.0 * (l - 1.0) ** 2 - 1.0, 1.0)
        )
        fresh = np.where(l < m, 0.0, np.where(l == m, diagonal, a * (x[None] * prev - b * before)))
        out[l] = fresh * weight[None]
        prev, before = fresh, prev
    return out


def legendre_table():
    basis = legendre_basis()
    table = np.zeros((SP, PAIRS, 256, SP, 8))
    for s in range(SP):
        for i in range(PAIRS):
            q = SP * i + s
            first = basis[q:, q].reshape(-1, SP, LOCAL_ROWS)
            second = basis[MMAX - 1 - q :, MMAX - 1 - q].reshape(-1, SP, LOCAL_ROWS)
            table[s, i, : MMAX - q, :, :LOCAL_ROWS] = first
            table[s, i, MMAX - q : MMAX + 1, :, :LOCAL_ROWS] = second
    both = split_np(table.reshape(SP, PAIRS, 256, 256))
    return np.ascontiguousarray(np.moveaxis(both, 0, 2))


def split(x):
    hi = x.astype(BF16)
    return hi, (x - hi.astype(F32)).astype(BF16)


def dot(a, b):
    return jnp.dot(a, b, preferred_element_type=F32)


def dot_t(a, b):
    return lax.dot_general(a, b, (((1,), (1,)), ((), ())), preferred_element_type=F32)


def three(product, a, b):
    return product(a[0], b[0]) + (product(a[1], b[0]) + product(a[0], b[1]))


def slope(diff):
    return diff * lax.rsqrt(diff * diff + 0.01)


def standardize(values):
    centred = values - jnp.mean(values, axis=-1, keepdims=True)
    return centred * lax.rsqrt(jnp.mean(centred * centred, axis=-1, keepdims=True) + 1e-05)


def kernel(
    emb_hbm, target_hbm, gain_hbm, head_hbm, fwd_hbm, back_hbm, leg_hbm,
    out_ref, out_gain_ref,
    emb_ref, target_ref, gain_ref, head_ref, fwd_ref, back_ref, leg_ref,
    feat_ref, grid_ref, waves_ref, third_ref, tall_ref,
    tsend, trecv, psend, precv, csend, crecv, ctruth, gsend, grecv, bsend, brecv,
    rsend, rrecv, esend, erecv, sums_ref,
    load_sem, send_sem, recv_sem,
):
    e = lax.axis_index("ens")
    s = lax.axis_index("sp")
    y, z_hi = e // 4, e % 4
    x, z_lo, core = s // 8, (s // 2) % 4, s % 2
    plane = y * 8 + x * 2 + core
    z = z_hi * 4 + z_lo

    def in_plane(d):
        to = (plane + d) % 32
        return to, ((to // 8) * 4 + z_hi, ((to // 2) % 4) * 8 + z_lo * 2 + to % 2)

    def along_z(d):
        to = (z + d) % 16
        return to, (y * 4 + to // 4, x * 8 + (to % 4) * 2 + core)

    barrier = pltpu.get_barrier_semaphore()

    def greet(device):
        pl.semaphore_signal(barrier, inc=1, device_id=device, device_id_type=MESH)

    def greet_ens(d, carry):
        greet(((e + d) % MEMBERS, s))
        return carry

    def greet_sp(d, carry):
        greet((e, (s + d) % SP))
        return carry

    def greet_z(d, carry):
        greet(
            (
                y * 4 + (z_hi + 1 + d // 3) % 4,
                x * 8 + ((z_lo + 1 + d % 3) % 4) * 2 + core,
            )
        )
        return carry

    def greet_plane(d, carry):
        to = (x * 2 + core + 1 + d % 7) % 8
        greet((((y + 1 + d // 7) % 4) * 4 + z_hi, (to // 2) * 8 + z_lo * 2 + to % 2))
        return carry

    loads = [
        pltpu.make_async_copy(source, dest, load_sem.at[at])
        for at, (source, dest) in enumerate(
            [
                (emb_hbm, emb_ref), (gain_hbm, gain_ref), (head_hbm, head_ref),
                (fwd_hbm, fwd_ref), (target_hbm, target_ref), (leg_hbm.at[s], leg_ref),
                (back_hbm, back_ref),
            ]
        )
    ]
    for load in loads:
        load.start()
    lax.fori_loop(1, MEMBERS, greet_ens, 0)
    lax.fori_loop(0, 9, greet_z, 0)
    lax.fori_loop(1, SP, greet_sp, 0)
    lax.fori_loop(0, 21, greet_plane, 0)

    lane = lax.broadcasted_iota(jnp.int32, (1, 128), 1)
    wide_lane = lax.broadcasted_iota(jnp.int32, (1, 256), 1)

    def turn(value, by):
        by = by % 128
        return pltpu.roll(value, by, 1) if by else value

    def grid_rows(row):
        at = 24 * row if row < 5 else 128
        return slice(at, at + 24)

    def to_waves():
        waves_ref[...] = three(dot_t, (fwd_ref[0], fwd_ref[1]), split(grid_ref[...]))

    def row_waves(row):
        group, start = (0, 24 * row) if row < 5 else (1, 0)
        parts = [
            turn(
                waves_ref[96 * hp : 96 * hp + 96, 128 * group : 128 * group + 128],
                24 * hp - start,
            )
            for hp in range(4)
        ]
        return jnp.where(
            lane < 48,
            jnp.where(lane < 24, parts[0], parts[1]),
            jnp.where(lane < 72, parts[2], parts[3]),
        )

    def every(row):
        return pl.ds(row, SP, stride=8)

    def quarter(row, value):
        return turn(value, 32 * (row % 4) - 64)

    def pack(blocks, buffer):
        rest = [jnp.zeros((SP, 128), F32), jnp.zeros((SP, 128), F32)]
        for row in range(LOCAL_ROWS):
            first, second, third = blocks(row)
            buffer[0, every(row), :] = jnp.where(lane < 96, first, turn(third, 96))
            buffer[1, every(row), :] = jnp.where(lane < 96, second, turn(third, 64))
            at = 32 * (row % 4)
            rest[row // 4] = jnp.where(
                (lane >= at) & (lane < at + 32), quarter(row, third), rest[row // 4]
            )
        buffer[0, every(6), :] = rest[0]
        buffer[0, every(7), :] = rest[1]

    def third_rows(buffer, row):
        return jnp.where(
            lane < 32,
            turn(buffer[0, every(row), :], 32),
            jnp.where(
                lane < 64,
                turn(buffer[1, every(row), :], 64),
                turn(buffer[0, every(6 + row // 4), :], 64 - 32 * (row % 4)),
            ),
        )

    def exchange_sp(source, dest, at):
        def send(d, carry):
            to = (s + d) % SP
            pltpu.make_async_remote_copy(
                src_ref=source.at[:, pl.ds(pl.multiple_of(8 * to, 8), 8), :],
                dst_ref=dest.at[:, pl.ds(pl.multiple_of(8 * s, 8), 8), :],
                send_sem=send_sem.at[at], recv_sem=recv_sem.at[at],
                device_id=(e, to), device_id_type=MESH,
            ).start()
            return carry

        lax.fori_loop(1, SP, send, 0)
        mine = pl.ds(pl.multiple_of(8 * s, 8), 8)
        dest[:, mine, :] = source[:, mine, :]

    def exchange_ens(source, dest, at):
        def send(d, carry):
            to = (e + d) % MEMBERS
            pltpu.make_async_remote_copy(
                src_ref=source.at[to], dst_ref=dest.at[e],
                send_sem=send_sem.at[at], recv_sem=recv_sem.at[at],
                device_id=(to, s), device_id_type=MESH,
            ).start()
            return carry

        lax.fori_loop(1, MEMBERS, send, 0)
        dest[e] = source[e]

    def settle(piece, sem):
        pltpu.make_async_copy(piece, piece, sem).wait()

    def sp_piece(ref):
        return ref.at[:, pl.ds(0, 8 * (SP - 1)), :]

    def ens_piece(ref):
        return ref.at[pl.ds(0, MEMBERS - 1)]

    grid_ref[...] = jnp.zeros((256, COLS), F32)
    psend[...] = jnp.zeros((2, 256, 128), F32)
    tsend[...] = jnp.zeros((1, 256, 128), F32)
    third_ref[...] = jnp.zeros((256, 128), F32)
    for load in loads[:3]:
        load.wait()
    gain = gain_ref[...]
    head = head_ref[...]

    def norm_chunk(at, carry):
        rows = pl.ds(pl.multiple_of(at * STEP, STEP), STEP)
        xhat = standardize(emb_ref[rows, :].astype(F32))
        feat_ref[rows, 0:256] = (xhat * gain).astype(BF16)
        return carry

    lax.fori_loop(0, POINTS // STEP, norm_chunk, 0)
    for row in range(LOCAL_ROWS):
        grid_ref[grid_rows(row), :] = dot_t(head, feat_ref[COLS * row : COLS * row + COLS, 0:256])
    loads[3].wait()
    to_waves()

    def pred_blocks(row):
        block = row_waves(row)
        return [block[SP * i : SP * i + SP] for i in range(PAIRS)]

    pack(pred_blocks, psend)
    pl.semaphore_wait(barrier, SP - 1 + MEMBERS - 1 + 9 + 21)
    exchange_sp(psend, precv, 1)

    loads[4].wait()
    for row in range(LOCAL_ROWS):
        grid_ref[grid_rows(row), :] = target_ref[row].astype(F32)
    to_waves()
    column = (e % 3) * 16
    for row in range(LOCAL_ROWS):
        block = pltpu.roll(row_waves(row), (128 - column) % 128, 1)
        merged = jnp.zeros((SP, 128), F32)
        for i in range(PAIRS):
            part = block[SP * i : SP * i + SP]
            for h in range(2):
                at = 32 * i + 16 * h
                merged = jnp.where(
                    (lane >= at) & (lane < at + 16), turn(part, at - 48 * h), merged
                )
        tsend[0, every(row), :] = merged
    exchange_sp(tsend, trecv, 0)

    def xhat_chunk(at, carry):
        rows = pl.ds(pl.multiple_of(at * STEP, STEP), STEP)
        hi, lo = split(standardize(emb_ref[rows, :].astype(F32)))
        feat_ref[rows, 256:512] = hi
        feat_ref[rows, 512:768] = lo
        return carry

    lax.fori_loop(0, POINTS // STEP, xhat_chunk, 0)
    loads[5].wait()
    loads[6].wait()

    def edge(i):
        return MMAX - (SP * i + s)

    def terms_of(i, fields):
        return three(dot, (leg_ref[i, 0], leg_ref[i, 1]), split(fields)).T

    def tail_groups(tails):
        third = jnp.where(lane < 65, tails[0], pltpu.roll(tails[1], 65, 1))
        fourth = jnp.where(
            lane < 65, tails[2], jnp.where(lane < 67, pltpu.roll(tails[1], 2, 1), 0.0)
        )
        return third, fourth

    settle(sp_piece(precv), recv_sem.at[1])
    for row in range(LOCAL_ROWS):
        third_ref[every(row), :] = third_rows(precv, row)
    tails = []
    for i, fields in enumerate((precv[0], precv[1], third_ref[...])):
        terms = terms_of(i, fields)
        packed = jnp.where(wide_lane < edge(i), terms[0:48], terms[48:96])
        for b in range(3):
            csend[3 * i + b] = packed[16 * b : 16 * b + 16, 0:128]
        tails.append(packed[:, 128:256])
    for c, group in enumerate(tail_groups(tails)):
        for b in range(3):
            csend[9 + 3 * c + b] = group[16 * b : 16 * b + 16]
    csend[15] = jnp.zeros((16, 128), F32)
    exchange_ens(csend, crecv, 2)

    settle(sp_piece(trecv), recv_sem.at[0])
    tails = []
    for i in range(PAIRS):
        terms = terms_of(i, trecv[0])
        packed = jnp.where(
            wide_lane < edge(i), terms[32 * i : 32 * i + 16], terms[32 * i + 16 : 32 * i + 32]
        )
        ctruth[i] = packed[:, 0:128]
        tails.append(packed[:, 128:256])
    ctruth[3], ctruth[4] = tail_groups(tails)
    ctruth[5] = jnp.zeros((16, 128), F32)
    truth = ctruth[e // 3]
    settle(ens_piece(crecv), recv_sem.at[2])

    members = crecv[...]

    def turned(value, by):
        by = by % MEMBERS
        return jnp.concatenate([value[MEMBERS - by :], value[: MEMBERS - by]], axis=0)

    pair = slope(members - turned(members, 8))
    for by in range(1, 8):
        term = slope(members - turned(members, by))
        pair = pair + (term - turned(term, -by))
    gsend[...] = slope(members - truth[None]) * (1.0 / (MEMBERS * LMAX)) - pair * (
        1.0 / (MEMBERS * (MEMBERS - 1) * LMAX)
    )
    exchange_ens(gsend, grecv, 3)
    settle(ens_piece(grecv), recv_sem.at[3])

    groups = [
        jnp.concatenate([grecv[3 * c + b] for b in range(3)], axis=0) for c in range(5)
    ]
    tails = [
        jnp.where(lane < 65, groups[3], 0.0),
        jnp.where(
            lane < 63,
            pltpu.roll(groups[3], 63, 1),
            jnp.where(lane < 65, pltpu.roll(groups[4], 126, 1), 0.0),
        ),
        jnp.where(lane < 65, groups[4], 0.0),
    ]
    for i in range(PAIRS):
        packed = jnp.concatenate([groups[i], tails[i]], axis=1)
        both = jnp.concatenate(
            [
                jnp.where(wide_lane < edge(i), packed, 0.0),
                jnp.where(wide_lane < edge(i), 0.0, packed),
                jnp.zeros((32, 256), F32),
            ],
            axis=0,
        )
        tall_ref[i] = three(dot, split(both), (leg_ref[i, 0], leg_ref[i, 1])).T
    bsend[1] = jnp.zeros((256, 128), F32)
    pack(lambda row: [tall_ref[i, every(row), :] for i in range(PAIRS)], bsend)
    exchange_sp(bsend, brecv, 4)
    settle(sp_piece(brecv), recv_sem.at[4])

    pieces = []
    for row in range(LOCAL_ROWS):
        block = jnp.concatenate(
            [
                brecv[0, every(row), :], brecv[1, every(row), :], third_rows(brecv, row),
                jnp.zeros((32, 128), F32),
            ],
            axis=0,
        ).T
        pieces.append(
            jnp.concatenate([block[24 * hp : 24 * hp + 24] for hp in range(4)], axis=1)
        )
    waves = jnp.concatenate(pieces, axis=0)
    gpred = three(dot, split(waves), (back_ref[0], back_ref[1]))
    flat = jnp.concatenate(
        [gpred[24 * row : 24 * row + 24] for row in range(LOCAL_ROWS)], axis=1
    ).astype(BF16)
    grads = dot(flat, feat_ref[...])
    gain_grad = jnp.sum(
        (grads[:, 256:512] + grads[:, 512:768]) * head.astype(F32), axis=0, keepdims=True
    )
    for v in range(NVAR):
        rsend[v] = grads[v : v + 1, 0:256]
    rsend[NVAR] = gain_grad
    for r in range(NVAR + 1, 32):
        rsend[r] = jnp.zeros((1, 256), F32)

    def scatter(d, carry):
        to, device = in_plane(d)
        pltpu.make_async_remote_copy(
            src_ref=rsend.at[to], dst_ref=rrecv.at[plane],
            send_sem=send_sem.at[5], recv_sem=recv_sem.at[5],
            device_id=device, device_id_type=MESH,
        ).start()
        return carry

    lax.fori_loop(1, 32, scatter, 0)
    rrecv[plane] = rsend[plane]
    settle(rrecv.at[pl.ds(0, 31)], recv_sem.at[5])
    total = rrecv[0]
    for r in range(1, 32):
        total = total + rrecv[r]
    esend[...] = total

    def spread(d, carry):
        _, device = along_z(d)
        pltpu.make_async_remote_copy(
            src_ref=esend, dst_ref=erecv.at[z],
            send_sem=send_sem.at[6], recv_sem=recv_sem.at[6],
            device_id=device, device_id_type=MESH,
        ).start()
        return carry

    lax.fori_loop(1, 16, spread, 0)
    erecv[z] = total
    settle(erecv.at[pl.ds(0, 15)], recv_sem.at[6])
    total = erecv[0]
    for r in range(1, 16):
        total = total + erecv[r]
    sums_ref[plane] = total

    def gather(d, carry):
        _, device = in_plane(d)
        pltpu.make_async_remote_copy(
            src_ref=sums_ref.at[plane], dst_ref=sums_ref.at[plane],
            send_sem=send_sem.at[7], recv_sem=recv_sem.at[7],
            device_id=device, device_id_type=MESH,
        ).start()
        return carry

    lax.fori_loop(1, 32, gather, 0)
    settle(sp_piece(psend), send_sem.at[1])
    settle(sp_piece(tsend), send_sem.at[0])
    settle(ens_piece(csend), send_sem.at[2])
    settle(ens_piece(gsend), send_sem.at[3])
    settle(sp_piece(bsend), send_sem.at[4])
    settle(rsend.at[pl.ds(0, 31)], send_sem.at[5])
    settle(erecv.at[pl.ds(0, 15)], send_sem.at[6])
    settle(sums_ref.at[pl.ds(0, 31)], recv_sem.at[7])
    for v in range(NVAR):
        out_ref[v : v + 1, :] = sums_ref[v]
    out_gain_ref[...] = sums_ref[NVAR]
    settle(sums_ref.at[pl.ds(0, 31)], send_sem.at[7])


def per_device(forward, back, legendre, embedding, target, gain, head_w):
    vmem = pl.BlockSpec(memory_space=pltpu.VMEM)
    hbm = pl.BlockSpec(memory_space=pltpu.HBM)
    ens_block = pltpu.VMEM((MEMBERS, 16, 128), F32)
    two = pltpu.VMEM((2, 256, 128), F32)
    one = pltpu.VMEM((1, 256, 128), F32)
    rows = pltpu.VMEM((32, 1, 256), F32)
    grad_head, grad_gain = pl.pallas_call(
        kernel,
        out_shape=(
            jax.ShapeDtypeStruct((NVAR, EMBED), F32), jax.ShapeDtypeStruct((1, EMBED), F32),
        ),
        in_specs=[hbm] * 7,
        out_specs=(vmem, vmem),
        scratch_shapes=[
            pltpu.VMEM((POINTS, EMBED), BF16),
            pltpu.VMEM((LOCAL_ROWS, NVAR, COLS), BF16),
            pltpu.VMEM((1, EMBED), F32),
            pltpu.VMEM((NVAR, EMBED), BF16),
            pltpu.VMEM((2, 384, COLS), BF16),
            pltpu.VMEM((2, 512, COLS), BF16),
            pltpu.VMEM((PAIRS, 2, 256, 256), BF16),
            pltpu.VMEM((POINTS, 3 * EMBED), BF16),
            pltpu.VMEM((256, COLS), F32),
            pltpu.VMEM((384, 256), F32),
            pltpu.VMEM((256, 128), F32),
            pltpu.VMEM((PAIRS, 256, 128), F32),
            one, one, two, two,
            ens_block, ens_block, pltpu.VMEM((6, 16, 128), F32), ens_block, ens_block,
            two, two,
            rows, rows,
            pltpu.VMEM((1, 256), F32),
            pltpu.VMEM((16, 1, 256), F32),
            rows,
            pltpu.SemaphoreType.DMA((7,)),
            pltpu.SemaphoreType.DMA((8,)),
            pltpu.SemaphoreType.DMA((8,)),
        ],
        compiler_params=pltpu.CompilerParams(
            collective_id=0, has_side_effects=True, vmem_limit_bytes=63 * 1024 * 1024
        ),
        name="crps",
    )(
        embedding.reshape(POINTS, EMBED), jnp.swapaxes(target, 0, 1), gain.reshape(1, EMBED),
        head_w.T, forward, back, legendre,
    )
    return grad_head.T, grad_gain.reshape(EMBED)


def solution(mesh):
    forward, back = dft_tables()
    legendre = legendre_table()
    in_specs = (P("ens", "sp", None, None), P(None, "sp", None), P(), P())

    def run(*args):
        return jax.shard_map(
            functools.partial(
                per_device, jnp.asarray(forward), jnp.asarray(back), jnp.asarray(legendre)
            ),
            mesh=mesh, in_specs=in_specs, out_specs=(P(), P()), check_vma=False,
        )(*args)

    return run
```

time: 95.5 us -> 80.1 us (0.84)
  Pallas kernels: 87.5 us -> 76.6 us
  local copies, waits for them, and re-layouts: 7.07 us -> 2.58 us
    pallas_call x1, Pallas kernels: 87.5 us -> 76.6 us  [per_device(): pl.pallas_call(kernel, out_shape=(jax.ShapeDtypeStruct((NVAR, EMBED), F32...]
    unnamed x11 -> x2, local copies, waits for them, and re-layouts: 6.5 us -> 2.58 us
where the time goes in v2:
time: 80.1 us; the launch traced here: 79.9 us
  Pallas kernels  76.6 us (96%)
  local copies, waits for them, and re-layouts  2.58 us (3%)
    pallas_call x1, Pallas kernels, per_device(): pl.pallas_call(kernel, out_shape=(jax.ShapeDtypeStruct((NVAR, EMBED), F32...  76.6 us
    unnamed x2, local copies, waits for them, and re-layouts  2.58 us

profile of v2, /device:TPU:1, one launch (start us, length us, event | category | flops | bytes accessed | tf_op | source)
XLA Modules:
  0.0 79.9 jit_solution(17702163299250262225)
XLA Ops:
  0.6 76.6 %crps.1 = (f32[24,256]{1,0:T(8,128)}, f32[1,256]{1,0:T(1,128)}) custom-call(bf16[2304,256]{1,0:T(8,128)(2,1)} %bitcast.6, bf16[6,24,384]{2,1,0:T(8,128)(2,1)} %bitcast.7, f32[1,256]{1,0:T(1,128)} %bitcast.10, bf16[24,256]{1,0:T(8,128)(2,1)} %bitcast.9, bf16[2,384,384]{2,1,0:T(8,128)(2,1)} %constant.6.clone.fwd_hbm, ...), custom_call_target="tpu_custom_call" | custom-call | tf_op jit(solution)/shard_map/crps/pallas_call | solution.py:517
  77.3 1.3 %copy.11 = f32[256,24]{0,1:T(8,128)} copy(f32[256,24]{0,1:T(8,128)} %bitcast.8) | data formatting | bytes 49152
  78.6 1.2 %copy.12 = f32[256]{0:T(256)} copy(f32[256]{0:T(256)} %bitcast.11) | data formatting | bytes 2048

commit v3 on v2

--- a/solution.py
+++ b/solution.py
@@ -113,6 +113,21 @@
     return centred * lax.rsqrt(jnp.mean(centred * centred, axis=-1, keepdims=True) + 1e-05)
 
 
+def far(n):
+    return (2 + n + n // 2 + 2 * (n // 3)) % 4
+
+
+def copy_kernel(head_in, gain_in, head_out, gain_out, sems):
+    copies = [
+        pltpu.make_async_copy(head_in, head_out, sems.at[0]),
+        pltpu.make_async_copy(gain_in, gain_out, sems.at[1]),
+    ]
+    for copy in copies:
+        copy.start()
+    for copy in copies:
+        copy.wait()
+
+
 def kernel(
     emb_hbm, target_hbm, gain_hbm, head_hbm, fwd_hbm, back_hbm, leg_hbm,
     out_ref, out_gain_ref,
@@ -129,25 +144,34 @@
     plane = y * 8 + x * 2 + core
     z = z_hi * 4 + z_lo
 
-    def in_plane(d):
-        to = (plane + d) % 32
-        return to, ((to // 8) * 4 + z_hi, ((to // 2) % 4) * 8 + z_lo * 2 + to % 2)
-
-    def along_z(d):
-        to = (z + d) % 16
-        return to, (y * 4 + to // 4, x * 8 + (to % 4) * 2 + core)
+    def in_plane(n):
+        to_y, to_x, to_core = (y + far(n // 8)) % 4, (x + far(n % 8 // 2)) % 4, (core + n + 1) % 2
+        return to_y * 8 + to_x * 2 + to_core, (to_y * 4 + z_hi, to_x * 8 + z_lo * 2 + to_core)
+
+    def along_z(n):
+        to = (z + 8 + (n + 1) // 2 * (1 - 2 * ((n + 1) % 2))) % 16
+        return to, (y * 4 + to // 4, x * 8 + to % 4 * 2 + core)
+
+    def in_sp(n):
+        to_z, to_x, to_core = (z_lo + far(n // 8)) % 4, (x + far(n % 8 // 2)) % 4, (core + n + 1) % 2
+        to = to_x * 8 + to_z * 2 + to_core
+        return to, (e, to)
+
+    def in_ens(n):
+        to = (y + far(n % 4)) % 4 * 4 + (z_hi + far(n // 4)) % 4
+        return to, (to, s)
 
     barrier = pltpu.get_barrier_semaphore()
 
     def greet(device):
         pl.semaphore_signal(barrier, inc=1, device_id=device, device_id_type=MESH)
 
-    def greet_ens(d, carry):
-        greet(((e + d) % MEMBERS, s))
-        return carry
-
-    def greet_sp(d, carry):
-        greet((e, (s + d) % SP))
+    def greet_ens(n, carry):
+        greet(in_ens(n)[1])
+        return carry
+
+    def greet_sp(n, carry):
+        greet(in_sp(n)[1])
         return carry
 
     def greet_z(d, carry):
@@ -176,9 +200,9 @@
     ]
     for load in loads:
         load.start()
-    lax.fori_loop(1, MEMBERS, greet_ens, 0)
+    lax.fori_loop(0, MEMBERS - 1, greet_ens, 0)
     lax.fori_loop(0, 9, greet_z, 0)
-    lax.fori_loop(1, SP, greet_sp, 0)
+    lax.fori_loop(0, SP - 1, greet_sp, 0)
     lax.fori_loop(0, 21, greet_plane, 0)
 
     lane = lax.broadcasted_iota(jnp.int32, (1, 128), 1)
@@ -210,8 +234,8 @@
             jnp.where(lane < 72, parts[2], parts[3]),
         )
 
-    def every(row):
-        return pl.ds(row, SP, stride=8)
+    def every(row, block=0):
+        return pl.ds(8 * block + row, SP, stride=16)
 
     def quarter(row, value):
         return turn(value, 32 * (row % 4) - 64)
@@ -220,66 +244,70 @@
         rest = [jnp.zeros((SP, 128), F32), jnp.zeros((SP, 128), F32)]
         for row in range(LOCAL_ROWS):
             first, second, third = blocks(row)
-            buffer[0, every(row), :] = jnp.where(lane < 96, first, turn(third, 96))
-            buffer[1, every(row), :] = jnp.where(lane < 96, second, turn(third, 64))
+            buffer[every(row), :] = jnp.where(lane < 96, first, turn(third, 96))
+            buffer[every(row, 1), :] = jnp.where(lane < 96, second, turn(third, 64))
             at = 32 * (row % 4)
             rest[row // 4] = jnp.where(
                 (lane >= at) & (lane < at + 32), quarter(row, third), rest[row // 4]
             )
-        buffer[0, every(6), :] = rest[0]
-        buffer[0, every(7), :] = rest[1]
+        buffer[every(6), :] = rest[0]
+        buffer[every(7), :] = rest[1]
 
     def third_rows(buffer, row):
         return jnp.where(
             lane < 32,
-            turn(buffer[0, every(row), :], 32),
+            turn(buffer[every(row), :], 32),
             jnp.where(
                 lane < 64,
-                turn(buffer[1, every(row), :], 64),
-                turn(buffer[0, every(6 + row // 4), :], 64 - 32 * (row % 4)),
+                turn(buffer[every(row, 1), :], 64),
+                turn(buffer[every(6 + row // 4), :], 64 - 32 * (row % 4)),
             ),
         )
 
     def exchange_sp(source, dest, at):
-        def send(d, carry):
-            to = (s + d) % SP
+        size = source.shape[0] // SP
+
+        def place(owner):
+            return pl.ds(pl.multiple_of(size * owner, size), size)
+
+        def send(n, carry):
+            to, device = in_sp(n)
             pltpu.make_async_remote_copy(
-                src_ref=source.at[:, pl.ds(pl.multiple_of(8 * to, 8), 8), :],
-                dst_ref=dest.at[:, pl.ds(pl.multiple_of(8 * s, 8), 8), :],
+                src_ref=source.at[place(to)],
+                dst_ref=dest.at[place(s)],
                 send_sem=send_sem.at[at], recv_sem=recv_sem.at[at],
-                device_id=(e, to), device_id_type=MESH,
+                device_id=device, device_id_type=MESH,
             ).start()
             return carry
 
-        lax.fori_loop(1, SP, send, 0)
-        mine = pl.ds(pl.multiple_of(8 * s, 8), 8)
-        dest[:, mine, :] = source[:, mine, :]
+        lax.fori_loop(0, SP - 1, send, 0)
+        dest[place(s), :] = source[place(s), :]
 
     def exchange_ens(source, dest, at):
-        def send(d, carry):
-            to = (e + d) % MEMBERS
+        def send(n, carry):
+            to, device = in_ens(n)
             pltpu.make_async_remote_copy(
                 src_ref=source.at[to], dst_ref=dest.at[e],
                 send_sem=send_sem.at[at], recv_sem=recv_sem.at[at],
-                device_id=(to, s), device_id_type=MESH,
+                device_id=device, device_id_type=MESH,
             ).start()
             return carry
 
-        lax.fori_loop(1, MEMBERS, send, 0)
+        lax.fori_loop(0, MEMBERS - 1, send, 0)
         dest[e] = source[e]
 
     def settle(piece, sem):
         pltpu.make_async_copy(piece, piece, sem).wait()
 
     def sp_piece(ref):
-        return ref.at[:, pl.ds(0, 8 * (SP - 1)), :]
+        return ref.at[pl.ds(0, ref.shape[0] // SP * (SP - 1))]
 
     def ens_piece(ref):
         return ref.at[pl.ds(0, MEMBERS - 1)]
 
     grid_ref[...] = jnp.zeros((256, COLS), F32)
-    psend[...] = jnp.zeros((2, 256, 128), F32)
-    tsend[...] = jnp.zeros((1, 256, 128), F32)
+    psend[...] = jnp.zeros((512, 128), F32)
+    tsend[...] = jnp.zeros((256, 128), F32)
     third_ref[...] = jnp.zeros((256, 128), F32)
     for load in loads[:3]:
         load.wait()
@@ -321,7 +349,7 @@
                 merged = jnp.where(
                     (lane >= at) & (lane < at + 16), turn(part, at - 48 * h), merged
                 )
-        tsend[0, every(row), :] = merged
+        tsend[pl.ds(row, SP, stride=8), :] = merged
     exchange_sp(tsend, trecv, 0)
 
     def xhat_chunk(at, carry):
@@ -350,9 +378,12 @@
 
     settle(sp_piece(precv), recv_sem.at[1])
     for row in range(LOCAL_ROWS):
-        third_ref[every(row), :] = third_rows(precv, row)
+        third_ref[pl.ds(row, SP, stride=8), :] = third_rows(precv, row)
     tails = []
-    for i, fields in enumerate((precv[0], precv[1], third_ref[...])):
+    blocks = precv[...].reshape(SP, 2, 8, 128)
+    for i, fields in enumerate(
+        (blocks[:, 0].reshape(256, 128), blocks[:, 1].reshape(256, 128), third_ref[...])
+    ):
         terms = terms_of(i, fields)
         packed = jnp.where(wide_lane < edge(i), terms[0:48], terms[48:96])
         for b in range(3):
@@ -367,7 +398,7 @@
     settle(sp_piece(trecv), recv_sem.at[0])
     tails = []
     for i in range(PAIRS):
-        terms = terms_of(i, trecv[0])
+        terms = terms_of(i, trecv[...])
         packed = jnp.where(
             wide_lane < edge(i), terms[32 * i : 32 * i + 16], terms[32 * i + 16 : 32 * i + 32]
         )
@@ -417,8 +448,8 @@
             axis=0,
         )
         tall_ref[i] = three(dot, split(both), (leg_ref[i, 0], leg_ref[i, 1])).T
-    bsend[1] = jnp.zeros((256, 128), F32)
-    pack(lambda row: [tall_ref[i, every(row), :] for i in range(PAIRS)], bsend)
+    bsend[...] = jnp.zeros((512, 128), F32)
+    pack(lambda row: [tall_ref[i, pl.ds(row, SP, stride=8), :] for i in range(PAIRS)], bsend)
     exchange_sp(bsend, brecv, 4)
     settle(sp_piece(brecv), recv_sem.at[4])
 
@@ -426,7 +457,7 @@
     for row in range(LOCAL_ROWS):
         block = jnp.concatenate(
             [
-                brecv[0, every(row), :], brecv[1, every(row), :], third_rows(brecv, row),
+                brecv[every(row), :], brecv[every(row, 1), :], third_rows(brecv, row),
                 jnp.zeros((32, 128), F32),
             ],
             axis=0,
@@ -449,8 +480,8 @@
     for r in range(NVAR + 1, 32):
         rsend[r] = jnp.zeros((1, 256), F32)
 
-    def scatter(d, carry):
-        to, device = in_plane(d)
+    def scatter(n, carry):
+        to, device = in_plane(n)
         pltpu.make_async_remote_copy(
             src_ref=rsend.at[to], dst_ref=rrecv.at[plane],
             send_sem=send_sem.at[5], recv_sem=recv_sem.at[5],
@@ -458,7 +489,7 @@
         ).start()
         return carry
 
-    lax.fori_loop(1, 32, scatter, 0)
+    lax.fori_loop(0, 31, scatter, 0)
     rrecv[plane] = rsend[plane]
     settle(rrecv.at[pl.ds(0, 31)], recv_sem.at[5])
     total = rrecv[0]
@@ -466,8 +497,8 @@
         total = total + rrecv[r]
     esend[...] = total
 
-    def spread(d, carry):
-        _, device = along_z(d)
+    def spread(n, carry):
+        _, device = along_z(n)
         pltpu.make_async_remote_copy(
             src_ref=esend, dst_ref=erecv.at[z],
             send_sem=send_sem.at[6], recv_sem=recv_sem.at[6],
@@ -475,7 +506,7 @@
         ).start()
         return carry
 
-    lax.fori_loop(1, 16, spread, 0)
+    lax.fori_loop(0, 15, spread, 0)
     erecv[z] = total
     settle(erecv.at[pl.ds(0, 15)], recv_sem.at[6])
     total = erecv[0]
@@ -483,8 +514,8 @@
         total = total + erecv[r]
     sums_ref[plane] = total
 
-    def gather(d, carry):
-        _, device = in_plane(d)
+    def gather(n, carry):
+        _, device = in_plane(n)
         pltpu.make_async_remote_copy(
             src_ref=sums_ref.at[plane], dst_ref=sums_ref.at[plane],
             send_sem=send_sem.at[7], recv_sem=recv_sem.at[7],
@@ -492,7 +523,7 @@
         ).start()
         return carry
 
-    lax.fori_loop(1, 32, gather, 0)
+    lax.fori_loop(0, 31, gather, 0)
     settle(sp_piece(psend), send_sem.at[1])
     settle(sp_piece(tsend), send_sem.at[0])
     settle(ens_piece(csend), send_sem.at[2])
@@ -511,8 +542,8 @@
     vmem = pl.BlockSpec(memory_space=pltpu.VMEM)
     hbm = pl.BlockSpec(memory_space=pltpu.HBM)
     ens_block = pltpu.VMEM((MEMBERS, 16, 128), F32)
-    two = pltpu.VMEM((2, 256, 128), F32)
-    one = pltpu.VMEM((1, 256, 128), F32)
+    two = pltpu.VMEM((512, 128), F32)
+    one = pltpu.VMEM((256, 128), F32)
     rows = pltpu.VMEM((32, 1, 256), F32)
     grad_head, grad_gain = pl.pallas_call(
         kernel,
@@ -553,6 +584,17 @@
         embedding.reshape(POINTS, EMBED), jnp.swapaxes(target, 0, 1), gain.reshape(1, EMBED),
         head_w.T, forward, back, legendre,
     )
+    grad_head, grad_gain = pl.pallas_call(
+        copy_kernel,
+        out_shape=(
+            jax.ShapeDtypeStruct((NVAR, EMBED), F32), jax.ShapeDtypeStruct((1, EMBED), F32),
+        ),
+        in_specs=[hbm, hbm],
+        out_specs=(hbm, hbm),
+        scratch_shapes=[pltpu.SemaphoreType.DMA((2,))],
+        compiler_params=pltpu.CompilerParams(vmem_limit_bytes=63 * 1024 * 1024),
+        name="results",
+    )(grad_head, grad_gain)
     return grad_head.T, grad_gain.reshape(EMBED)
 
 

time: 80.1 us -> 76.8 us (0.959)
  local copies, waits for them, and re-layouts: 2.58 us -> 0 us
    unnamed x2 -> x0, local copies, waits for them, and re-layouts: 2.58 us -> none
    pallas_call x1, Pallas kernels: 76.6 us -> 74.1 us  [per_device(): pl.pallas_call(kernel, out_shape=(jax.ShapeDtypeStruct((NVAR, EMBED), F32...]
    pallas_call x0 -> x1, Pallas kernels: none -> 1.9 us  [per_device(): pl.pallas_call(copy_kernel, out_shape=(jax.ShapeDtypeStruct((NVAR, EMBED)...]
where the time goes in v3:
time: 76.8 us; the launch traced here: 76.7 us
  Pallas kernels  76 us (99%)
    pallas_call x1, Pallas kernels, per_device(): pl.pallas_call(kernel, out_shape=(jax.ShapeDtypeStruct((NVAR, EMBED), F32...  74.1 us
    pallas_call x1, Pallas kernels, per_device(): pl.pallas_call(copy_kernel, out_shape=(jax.ShapeDtypeStruct((NVAR, EMBED)...  1.9 us

profile of v3, /device:TPU:1, one launch (start us, length us, event | category | flops | bytes accessed | tf_op | source)
XLA Modules:
  0.0 76.7 jit_solution(13859412154210415299)
XLA Ops:
  0.6 74.1 %crps.1 = (f32[24,256]{1,0:T(8,128)}, f32[1,256]{1,0:T(1,128)}) custom-call(bf16[2304,256]{1,0:T(8,128)(2,1)} %bitcast.6, bf16[6,24,384]{2,1,0:T(8,128)(2,1)} %bitcast.7, f32[1,256]{1,0:T(1,128)} %bitcast.9, bf16[24,256]{1,0:T(8,128)(2,1)} %bitcast.8, bf16[2,384,384]{2,1,0:T(8,128)(2,1)} %constant.6.clone.fwd_hbm, ...), custom_call_target="tpu_custom_call" | custom-call | tf_op jit(solution)/shard_map/crps/pallas_call | solution.py:548
  74.8 1.9 %results.1 = (f32[24,256]{1,0:T(8,128)}, f32[1,256]{1,0:T(1,128)}) custom-call(f32[24,256]{1,0:T(8,128)} %get-tuple-element.6.head_in, f32[1,256]{1,0:T(1,128)} %get-tuple-element.7.gain_in), custom_call_target="tpu_custom_call" | custom-call | tf_op jit(solution)/shard_map/results/pallas_call | solution.py:587

commit v4 on v3

--- a/solution.py
+++ b/solution.py
@@ -200,10 +200,10 @@
     ]
     for load in loads:
         load.start()
-    lax.fori_loop(0, MEMBERS - 1, greet_ens, 0)
-    lax.fori_loop(0, 9, greet_z, 0)
-    lax.fori_loop(0, SP - 1, greet_sp, 0)
-    lax.fori_loop(0, 21, greet_plane, 0)
+    lax.fori_loop(0, MEMBERS - 1, greet_ens, 0, unroll=True)
+    lax.fori_loop(0, 9, greet_z, 0, unroll=True)
+    lax.fori_loop(0, SP - 1, greet_sp, 0, unroll=True)
+    lax.fori_loop(0, 21, greet_plane, 0, unroll=True)
 
     lane = lax.broadcasted_iota(jnp.int32, (1, 128), 1)
     wide_lane = lax.broadcasted_iota(jnp.int32, (1, 256), 1)
@@ -280,7 +280,7 @@
             ).start()
             return carry
 
-        lax.fori_loop(0, SP - 1, send, 0)
+        lax.fori_loop(0, SP - 1, send, 0, unroll=True)
         dest[place(s), :] = source[place(s), :]
 
     def exchange_ens(source, dest, at):
@@ -293,7 +293,7 @@
             ).start()
             return carry
 
-        lax.fori_loop(0, MEMBERS - 1, send, 0)
+        lax.fori_loop(0, MEMBERS - 1, send, 0, unroll=True)
         dest[e] = source[e]
 
     def settle(piece, sem):
@@ -489,7 +489,7 @@
         ).start()
         return carry
 
-    lax.fori_loop(0, 31, scatter, 0)
+    lax.fori_loop(0, 31, scatter, 0, unroll=True)
     rrecv[plane] = rsend[plane]
     settle(rrecv.at[pl.ds(0, 31)], recv_sem.at[5])
     total = rrecv[0]
@@ -506,7 +506,7 @@
         ).start()
         return carry
 
-    lax.fori_loop(0, 15, spread, 0)
+    lax.fori_loop(0, 15, spread, 0, unroll=True)
     erecv[z] = total
     settle(erecv.at[pl.ds(0, 15)], recv_sem.at[6])
     total = erecv[0]
@@ -523,7 +523,7 @@
         ).start()
         return carry
 
-    lax.fori_loop(0, 31, gather, 0)
+    lax.fori_loop(0, 31, gather, 0, unroll=True)
     settle(sp_piece(psend), send_sem.at[1])
     settle(sp_piece(tsend), send_sem.at[0])
     settle(ens_piece(csend), send_sem.at[2])

time: 76.8 us -> 74.7 us (0.973)
  Pallas kernels: 76 us -> 73.9 us
    pallas_call x1, Pallas kernels: 74.1 us -> 72 us  [per_device(): pl.pallas_call(kernel, out_shape=(jax.ShapeDtypeStruct((NVAR, EMBED), F32...]
where the time goes in v4:
time: 74.7 us; the launch traced here: 74.6 us
  Pallas kernels  73.9 us (99%)
    pallas_call x1, Pallas kernels, per_device(): pl.pallas_call(kernel, out_shape=(jax.ShapeDtypeStruct((NVAR, EMBED), F32...  72 us
    pallas_call x1, Pallas kernels, per_device(): pl.pallas_call(copy_kernel, out_shape=(jax.ShapeDtypeStruct((NVAR, EMBED)...  1.9 us

profile of v4, /device:TPU:1, one launch (start us, length us, event | category | flops | bytes accessed | tf_op | source)
XLA Modules:
  0.0 74.6 jit_solution(13723887966497593588)
XLA Ops:
  0.6 72.0 %crps.1 = (f32[24,256]{1,0:T(8,128)}, f32[1,256]{1,0:T(1,128)}) custom-call(bf16[2304,256]{1,0:T(8,128)(2,1)} %bitcast.6, bf16[6,24,384]{2,1,0:T(8,128)(2,1)} %bitcast.7, f32[1,256]{1,0:T(1,128)} %bitcast.9, bf16[24,256]{1,0:T(8,128)(2,1)} %bitcast.8, bf16[2,384,384]{2,1,0:T(8,128)(2,1)} %constant.6.clone.fwd_hbm, ...), custom_call_target="tpu_custom_call" | custom-call | tf_op jit(solution)/shard_map/crps/pallas_call | solution.py:548
  72.7 1.9 %results.1 = (f32[24,256]{1,0:T(8,128)}, f32[1,256]{1,0:T(1,128)}) custom-call(f32[24,256]{1,0:T(8,128)} %get-tuple-element.6.head_in, f32[1,256]{1,0:T(1,128)} %get-tuple-element.7.gain_in), custom_call_target="tpu_custom_call" | custom-call | tf_op jit(solution)/shard_map/results/pallas_call | solution.py:587
